TPU v7x, 128 devices: a whole 4x4x4 slice. The times are simulated.
128 devices in a mesh: ctx: 32 (over z_lo, x, y), tp: 4 (over z_hi, core).
Axes of the slice: x: 4, y: 4, z: 4 (z_hi: 2, z_lo: 2; z = z_hi * 2 + z_lo), core: 2. Of those that a mesh axis runs over, the one named last changes fastest.
Arguments:
- queries: bfloat16 [8192, 4096], P('ctx', 'tp'), may hold values from -6 to 6
- attn_keys: bfloat16 [8192, 4096], P('ctx', 'tp'), may hold values from -6 to 6
- attn_values: bfloat16 [8192, 4096], P('ctx', 'tp'), may hold values from -6 to 6
- out_proj: bfloat16 [4096, 8192], P('tp'), may hold values from -0.25 to 0.25
Outputs:
- mixed: bfloat16 [8192, 8192], P('ctx', 'tp')
All inputs are finite; a program needn't handle non-finite values.
Results may differ from a plain program's by a relative error of at most 0.013.
Values may be sent and summed in bfloat16 or wider, within the bound.
A program may use at most 256 MiB of HBM per device.

v0:
```python
import jax
import jax.numpy as jnp
from jax import lax
from jax.sharding import PartitionSpec as P

HS = 128


def attend(carry, query_set, query_pos, key_piece, value_piece, key_pos):
    run_max, run_sum, run_acc = carry
    pieces = key_piece.shape[0]
    heads_local = query_set.shape[1]
    key_heads = key_piece.reshape(pieces, heads_local, HS)
    value_heads = value_piece.reshape(pieces, heads_local, HS)
    scores = jnp.einsum("rhd,phd->hrp", query_set, key_heads, preferred_element_type=jnp.float32)
    scores = scores * (1.0 / HS**0.5)
    visible = key_pos[None, None, :] <= query_pos[None, :, None]
    scores = jnp.where(visible, scores, -1e30)
    new_max = jnp.maximum(run_max, jnp.max(scores, axis=2))
    weights = jnp.where(visible, jnp.exp(scores - new_max[:, :, None]), 0.0)
    new_sum = jnp.sum(weights, axis=2)
    update = jnp.einsum(
        "hrp,phd->rhd",
        weights.astype(jnp.bfloat16),
        value_heads,
        preferred_element_type=jnp.float32,
    )
    return (new_max, new_sum, update)


def start_carry(heads_local, rows_count):
    return (
        jnp.full((heads_local, rows_count), -1e30, jnp.float32),
        jnp.zeros((heads_local, rows_count), jnp.float32),
        jnp.zeros((rows_count, heads_local, HS), jnp.float32),
    )


def body(queries, attn_keys, attn_values, out_proj):
    ctx_count = lax.axis_size("ctx")
    ctx_index = lax.axis_index("ctx")
    tok_dev = queries.shape[0]
    half_len = tok_dev // 2
    heads_local = queries.shape[1] // HS
    query_heads = queries.reshape(tok_dev, heads_local, HS)
    offsets = jnp.arange(half_len, dtype=jnp.int32)
    query_pos = jnp.concatenate(
        [ctx_index * half_len + offsets, (2 * ctx_count - 1 - ctx_index) * half_len + offsets]
    )
    key_piece = lax.all_gather(attn_keys, "ctx", axis=0, tiled=True)
    value_piece = lax.all_gather(attn_values, "ctx", axis=0, tiled=True)
    stored = jnp.arange(key_piece.shape[0], dtype=jnp.int32)
    device = stored // tok_dev
    within = stored % tok_dev
    key_pos = jnp.where(
        within < half_len,
        device * half_len + within,
        (2 * ctx_count - 1 - device) * half_len + within - half_len,
    )
    run_max, run_sum, run_acc = attend(
        start_carry(heads_local, tok_dev), query_heads, query_pos, key_piece, value_piece, key_pos
    )
    attended = (run_acc / jnp.transpose(run_sum)[:, :, None]).reshape(tok_dev, heads_local * HS)
    attended = attended.astype(jnp.bfloat16)
    partial_value = jnp.dot(attended, out_proj, preferred_element_type=jnp.float32).astype(
        jnp.bfloat16
    )
    share = lax.psum_scatter(
        partial_value.astype(jnp.float32).astype(jnp.bfloat16),
        "tp",
        scatter_dimension=1,
        tiled=True,
    )
    return share


def solution(mesh):
    in_specs = (P("ctx", "tp"), P("ctx", "tp"), P("ctx", "tp"), P("tp", None))
    out_specs = P("ctx", "tp")
    return jax.shard_map(body, mesh=mesh, in_specs=in_specs, out_specs=out_specs, check_vma=False)
```

profile of v0, /device:TPU:1, one launch (start us, length us, event | category | flops | bytes accessed | tf_op | source)
XLA Modules:
  0.0 570.7 jit_solution(6408303022841652659)
XLA Ops:
  6.5 0.0 copy-start
  6.5 0.0 all-gather.3.cloned.1.call-start
  6.5 2.1 copy.7
  8.6 0.0 all-gather.3.cloned.1.call-update
  8.7 0.0 all-gather.5.cloned.1.call-start
  8.7 0.7 all-gather.5.cloned.1.call-update
  9.4 0.0 reduce-scatter.2.cloned.1.call-start
  9.5 1.2 broadcast_compare_fusion
  10.7 224.2 %all-gather.3.cloned.1.call-done = bf16[8192,1024]{0,1:T(8,128)(2,1)} async-done(((bf16[256,1024]{0,1:T(8,128)(2,1)}), bf16[8192,1024]{0,1:T(8,128)(2,1)}) %all-gather.3.cloned.1.call-update) | async-done | bytes 16777232 | tf_op jit(solution)/shard_map/all_gather | solution.py:50
  235.0 0.0 copy-done
  235.0 31.6 %fusion = (f32[8,256]{1,0:T(8,128)S(1)}, f32[8,256,8192]{2,1,0:T(8,128)}) fusion(pred[256,8192]{1,0:T(8,128)(4,1)S(1)} %broadcast_compare_fusion, bf16[8192,8,128]{0,2,1:T(8,128)(2,1)} %bitcast.24, bf16[256,1024]{1,0:T(8,128)(2,1)S(1)} %copy-done), kind=kOutput, calls=%fused_computation.2 | convolution fusion | flops 4345296896 | bytes 86515712 | tf_op jit(solution)/shard_map/rhd,phd->hrp/dot_general | solution.py:15
  266.6 24.2 %fusion.1 = f32[8,256]{1,0:T(8,128)S(1)} fusion(f32[8,256,8192]{2,1,0:T(8,128)} %get-tuple-element.6, f32[8,256]{1,0:T(8,128)S(1)} %broadcast_maximum_fusion, pred[256,8192]{1,0:T(8,128)(4,1)S(1)} %broadcast_compare_fusion), kind=kLoop, calls=%fused_computation.3 | loop fusion | flops 83884032 | bytes 69222400 | tf_op jit(solution)/shard_map/reduce_sum | solution.py:21
  290.8 154.4 %all-gather.5.cloned.1.call-done = bf16[8192,1024]{1,0:T(8,128)(2,1)} async-done(((bf16[256,1024]{1,0:T(8,128)(2,1)}), bf16[8192,1024]{1,0:T(8,128)(2,1)}) %all-gather.5.cloned.1.call-update) | async-done | bytes 16777232 | tf_op jit(solution)/shard_map/all_gather | solution.py:51
  445.1 21.2 %copy.10 = bf16[8192,1024]{0,1:T(8,128)(2,1)} copy(bf16[8192,1024]{1,0:T(8,128)(2,1)} %all-gather.5.cloned.1.call-done) | data formatting | bytes 33554432 | tf_op jit(solution)/shard_map/all_gather | solution.py:51
  466.3 0.0 copy-start.1
  466.3 29.6 %divide_convert_fusion = bf16[256,8,128]{0,2,1:T(8,128)(2,1)S(1)} fusion(bf16[8192,8,128]{0,2,1:T(8,128)(2,1)} %bitcast.21, f32[8,256,8192]{2,1,0:T(8,128)} %get-tuple-element.6, f32[8,256]{1,0:T(8,128)S(1)} %broadcast_maximum_fusion, pred[256,8192]{1,0:T(8,128)(4,1)S(1)} %broadcast_compare_fusion, f32[256,8]{0,1:T(8,128)S(1)} %bitcast.23), kind=kOutput, calls=%fused_computation.10 | convolution fusion | flops 4379377664 | bytes 86523904 | tf_op jit(solution)/shard_map/hrp,phd->rhd/dot_general | solution.py:22
  496.0 12.2 %convolution_convert_fusion = bf16[256,8192]{1,0:T(8,128)(2,1)} fusion(bf16[256,1024]{0,1:T(8,128)(2,1)S(1)} %bitcast.22, bf16[1024,8192]{1,0:T(8,128)(2,1)} %param.7), kind=kOutput, calls=%fused_computation.7 | convolution fusion | flops 4297064448 | bytes 21495808 | tf_op jit(solution)/shard_map/dot_general | solution.py:65
  508.2 0.0 reduce-scatter.2.cloned.1.call-update
  508.2 55.9 %reduce-scatter.2.cloned.1.call-done = bf16[256,2048]{1,0:T(8,128)(2,1)} async-done(((bf16[256,8192]{1,0:T(8,128)(2,1)}), bf16[256,2048]{1,0:T(8,128)(2,1)}) %reduce-scatter.2.cloned.1.call-update) | async-done | bytes 1048592 | tf_op jit(solution)/shard_map/reduce_scatter | solution.py:68
  564.1 0.0 copy-done.1
  (4 shorter events, 0.0 us)
Async XLA Ops:
  6.5 228.4 %copy-start = (bf16[256,1024]{1,0:T(8,128)(2,1)S(1)}, bf16[256,1024]{1,0:T(8,128)(2,1)}, u32[]{:S(2)}) copy-start(bf16[256,1024]{1,0:T(8,128)(2,1)} %param.4) | copy-start | bytes 1572868
  6.5 228.4 %all-gather.3.cloned.1.call-start = ((), (), s32[]{:S(2)}) async-start(), calls=%async_computation.1 | async-start | bytes 17301504 | tf_op jit(solution)/shard_map/all_gather | solution.py:50
  8.7 436.5 %all-gather.5.cloned.1.call-start = ((), (), s32[]{:S(2)}) async-start(), calls=%async_computation.2 | async-start | bytes 17301504 | tf_op jit(solution)/shard_map/all_gather | solution.py:51
  9.4 554.7 %reduce-scatter.2.cloned.1.call-start = ((), (), s32[]{:S(2)}) async-start(), calls=%async_computation.3 | async-start | bytes 5242880 | tf_op jit(solution)/shard_map/reduce_scatter | solution.py:68
  466.3 97.8 %copy-start.1 = (bf16[256,1024]{1,0:T(8,128)(2,1)S(1)}, bf16[256,1024]{1,0:T(8,128)(2,1)}, u32[]{:S(2)}) copy-start(bf16[256,1024]{1,0:T(8,128)(2,1)} %param.4) | copy-start | bytes 1572868
Sparse Core Ops, SparseCore 0:
  8.9 225.9 all-gather.2
  236.6 208.4 all-gather.4
  508.4 55.7 reduce-scatter.1
where the time goes:
time: 571 us
  waiting for transfers between devices  435 us (76%)
  matrix products  73.5 us (13%)
  other arithmetic  25.4 us (4%)
  local copies, waits for them, and re-layouts  23.3 us (4%)
  between operations  13.2 us (2%)
    all_gather x1, waiting for transfers between devices, body(): key_piece = lax.all_gather(attn_keys, 'ctx', axis=0, tiled=True)  224 us
    all_gather x1, waiting for transfers between devices, body(): value_piece = lax.all_gather(attn_values, 'ctx', axis=0, tiled=True)  154 us
    reduce_scatter x1, waiting for transfers between devices, body(): lax.psum_scatter(partial_value.astype(jnp.float32).astype(jnp.bfloat16),...  55.9 us
    dot_general x1, matrix products, attend(): jnp.einsum('rhd,phd->hrp', query_set, key_heads, preferred_element_type=j...  31.6 us
    dot_general x1, matrix products, attend(): jnp.einsum('hrp,phd->rhd', weights.astype(jnp.bfloat16), value_heads, pre...  29.6 us
    reduce_sum x1, other arithmetic, attend(): new_sum = jnp.sum(weights, axis=2)  24.2 us
    all_gather x1, local copies, waits for them, and re-layouts, body(): value_piece = lax.all_gather(attn_values, 'ctx', axis=0, tiled=True)  21.2 us
    dot_general x1, matrix products, body(): jnp.dot(attended, out_proj, preferred_element_type=jnp.float32)  12.2 us
  transfers between devices with their start and end apart: 3, of which 3 were waited for; matrix products, arithmetic and copies ran while one was open for 10% of the time, Pallas kernels for 0%

commit v1 on v0

--- a/solution.py
+++ b/solution.py
@@ -47,8 +47,13 @@
     query_pos = jnp.concatenate(
         [ctx_index * half_len + offsets, (2 * ctx_count - 1 - ctx_index) * half_len + offsets]
     )
-    key_piece = lax.all_gather(attn_keys, "ctx", axis=0, tiled=True)
-    value_piece = lax.all_gather(attn_values, "ctx", axis=0, tiled=True)
+    key_piece, value_piece = jnp.split(
+        lax.all_gather(
+            jnp.concatenate([attn_keys, attn_values], axis=1), "ctx", axis=0, tiled=True
+        ),
+        [attn_keys.shape[1]],
+        axis=1,
+    )
     stored = jnp.arange(key_piece.shape[0], dtype=jnp.int32)
     device = stored // tok_dev
     within = stored % tok_dev

time: 571 us -> 590 us (1.033)
  waiting for transfers between devices: 435 us -> 452 us
    split x0 -> x1, local copies, waits for them, and re-layouts: none -> 23.1 us  [body(): jnp.split(lax.all_gather(jnp.concatenate([attn_keys, attn_values], axis=1...]
    all_gather x1 -> x0, local copies, waits for them, and re-layouts: 21.2 us -> none  [body(): value_piece = lax.all_gather(attn_values, 'ctx', axis=0, tiled=True)]
    reduce_scatter x1, waiting for transfers between devices: 55.9 us -> 74.5 us  [body(): lax.psum_scatter(partial_value.astype(jnp.float32).astype(jnp.bfloat16),...]
    all_gather x2 -> x1, waiting for transfers between devices: 379 us -> 378 us  [body(): lax.all_gather(jnp.concatenate([attn_keys, attn_values], axis=1), 'ctx',...]
  transfers between devices with their start and end apart: 3 -> 2, of which waited for: 3 -> 2; matrix products, arithmetic and copies ran while one was open for 10% -> 1% of each run, Pallas kernels for 0% -> 0%
where the time goes in v1:
time: 590 us; the launch traced here: 589 us
  waiting for transfers between devices  452 us (77%)
  matrix products  71.5 us (12%)
  other arithmetic  26.5 us (4%)
  local copies, waits for them, and re-layouts  25.7 us (4%)
  between operations  13.5 us (2%)
    all_gather x1, waiting for transfers between devices, body(): lax.all_gather(jnp.concatenate([attn_keys, attn_values], axis=1), 'ctx',...  378 us
    reduce_scatter x1, waiting for transfers between devices, body(): lax.psum_scatter(partial_value.astype(jnp.float32).astype(jnp.bfloat16),...  74.5 us
    dot_general x1, matrix products, attend(): jnp.einsum('hrp,phd->rhd', weights.astype(jnp.bfloat16), value_heads, pre...  29.6 us
    dot_general x1, matrix products, attend(): jnp.einsum('rhd,phd->hrp', query_set, key_heads, preferred_element_type=j...  29.6 us
    split x1, local copies, waits for them, and re-layouts, body(): jnp.split(lax.all_gather(jnp.concatenate([attn_keys, attn_values], axis=1...  23.1 us
    reduce_sum x1, other arithmetic, attend(): new_sum = jnp.sum(weights, axis=2)  21.7 us
    dot_general x1, matrix products, body(): jnp.dot(attended, out_proj, preferred_element_type=jnp.float32)  12.2 us
  transfers between devices with their start and end apart: 2, of which 2 were waited for; matrix products, arithmetic and copies ran while one was open for 1% of the time, Pallas kernels for 0%

profile of v1, /device:TPU:1, one launch (start us, length us, event | category | flops | bytes accessed | tf_op | source)
XLA Modules:
  0.0 589.3 jit_solution(7470514190447550688)
XLA Ops:
  6.5 0.0 copy-start
  6.5 0.0 all-gather.2.cloned.1.call-start
  6.5 1.3 copy.8
  7.8 1.2 copy.9
  9.1 1.0 pad_maximum_fusion
  10.1 0.0 all-gather.2.cloned.1.call-update
  10.2 0.0 reduce-scatter.2.cloned.1.call-start
  10.3 3.7 broadcast_compare_fusion
  14.0 377.7 %all-gather.2.cloned.1.call-done = bf16[8192,2048]{0,1:T(8,128)(2,1)} async-done(((bf16[256,2048]{0,1:T(8,128)(2,1)}), bf16[8192,2048]{0,1:T(8,128)(2,1)}) %all-gather.2.cloned.1.call-update) | async-done | bytes 33554448 | tf_op jit(solution)/shard_map/all_gather | solution.py:51
  391.7 23.1 %fusion.32 = (bf16[8192,1024]{0,1:T(8,128)(2,1)}, bf16[8192,1024]{0,1:T(8,128)(2,1)}) fusion(bf16[8192,2048]{0,1:T(8,128)(2,1)} %all-gather.2.cloned.1.call-done), kind=kLoop, calls=%fused_computation.41 | loop fusion | bytes 67108864 | tf_op jit(solution)/shard_map/split | solution.py:50
  414.8 0.0 copy-done
  414.8 29.6 %fusion = (f32[8,256]{1,0:T(8,128)S(1)}, f32[8,8192,256]{2,1,0:T(8,128)}) fusion(pred[256,8192]{0,1:T(8,128)(4,1)S(1)} %broadcast_compare_fusion, bf16[8192,8,128]{0,2,1:T(8,128)(2,1)} %bitcast.37, bf16[256,1024]{1,0:T(8,128)(2,1)S(1)} %copy-done), kind=kOutput, calls=%fused_computation.2 | convolution fusion | flops 4345296896 | bytes 86515712 | tf_op jit(solution)/shard_map/rhd,phd->hrp/dot_general | solution.py:15
  444.4 21.7 %fusion.1 = f32[8,256]{1,0:T(8,128)S(1)} fusion(f32[8,8192,256]{2,1,0:T(8,128)} %get-tuple-element.8, f32[8,256]{1,0:T(8,128)S(1)} %broadcast_maximum_fusion, pred[256,8192]{0,1:T(8,128)(4,1)S(1)} %broadcast_compare_fusion), kind=kLoop, calls=%fused_computation.3 | loop fusion | flops 83884032 | bytes 69222400 | tf_op jit(solution)/shard_map/reduce_sum | solution.py:21
  466.1 0.0 copy-start.1
  466.1 29.6 %divide_convert_fusion = bf16[256,8,128]{0,2,1:T(8,128)(2,1)S(1)} fusion(bf16[8192,8,128]{0,2,1:T(8,128)(2,1)} %bitcast.36, f32[8,8192,256]{2,1,0:T(8,128)} %get-tuple-element.8, f32[8,256]{1,0:T(8,128)S(1)} %broadcast_maximum_fusion, pred[256,8192]{0,1:T(8,128)(4,1)S(1)} %broadcast_compare_fusion, f32[256,8]{0,1:T(8,128)S(1)} %bitcast.39), kind=kOutput, calls=%fused_computation.11 | convolution fusion | flops 4379377664 | bytes 86523904 | tf_op jit(solution)/shard_map/hrp,phd->rhd/dot_general | solution.py:22
  495.8 12.2 %convolution_convert_fusion = bf16[256,8192]{1,0:T(8,128)(2,1)} fusion(bf16[256,1024]{0,1:T(8,128)(2,1)S(1)} %bitcast.38, bf16[1024,8192]{1,0:T(8,128)(2,1)} %param.7), kind=kOutput, calls=%fused_computation.7 | convolution fusion | flops 4297064448 | bytes 21495808 | tf_op jit(solution)/shard_map/dot_general | solution.py:70
  508.0 0.0 reduce-scatter.2.cloned.1.call-update
  508.0 74.5 %reduce-scatter.2.cloned.1.call-done = bf16[256,2048]{1,0:T(8,128)(2,1)} async-done(((bf16[256,8192]{1,0:T(8,128)(2,1)}), bf16[256,2048]{1,0:T(8,128)(2,1)}) %reduce-scatter.2.cloned.1.call-update) | async-done | bytes 1048592 | tf_op jit(solution)/shard_map/reduce_scatter | solution.py:73
  582.5 0.0 copy-done.1
  (4 shorter events, 0.0 us)
Async XLA Ops:
  6.5 408.3 %copy-start = (bf16[256,1024]{1,0:T(8,128)(2,1)S(1)}, bf16[256,1024]{1,0:T(8,128)(2,1)}, u32[]{:S(2)}) copy-start(bf16[256,1024]{1,0:T(8,128)(2,1)} %param.4) | copy-start | bytes 1572868
  6.5 385.2 %all-gather.2.cloned.1.call-start = ((), (), s32[]{:S(2)}) async-start(), calls=%async_computation.1 | async-start | bytes 34603008 | tf_op jit(solution)/shard_map/all_gather | solution.py:51
  10.2 572.3 %reduce-scatter.2.cloned.1.call-start = ((), (), s32[]{:S(2)}) async-start(), calls=%async_computation.2 | async-start | bytes 5242880 | tf_op jit(solution)/shard_map/reduce_scatter | solution.py:73
  466.1 116.4 %copy-start.1 = (bf16[256,1024]{1,0:T(8,128)(2,1)S(1)}, bf16[256,1024]{1,0:T(8,128)(2,1)}, u32[]{:S(2)}) copy-start(bf16[256,1024]{1,0:T(8,128)(2,1)} %param.4) | copy-start | bytes 1572868
Sparse Core Ops, SparseCore 0:
  10.3 381.3 all-gather.1
  508.1 74.3 reduce-scatter.1

commit v2 on v0

--- a/solution.py
+++ b/solution.py
@@ -47,7 +47,9 @@
     query_pos = jnp.concatenate(
         [ctx_index * half_len + offsets, (2 * ctx_count - 1 - ctx_index) * half_len + offsets]
     )
-    key_piece = lax.all_gather(attn_keys, "ctx", axis=0, tiled=True)
+    key_piece = jnp.concatenate(
+        lax.all_to_all(jnp.stack([attn_keys] * lax.axis_size("ctx")), "ctx", 0, 0), axis=0
+    )
     value_piece = lax.all_gather(attn_values, "ctx", axis=0, tiled=True)
     stored = jnp.arange(key_piece.shape[0], dtype=jnp.int32)
     device = stored // tok_dev

time: 571 us -> 598 us (1.047)
  local copies, waits for them, and re-layouts: 23.3 us -> 43.8 us
  starting transfers between devices: 0.08 us -> 9.39 us
    all_to_all x0 -> x1, waiting for transfers between devices: none -> 309 us  [body(): lax.all_to_all(jnp.stack([attn_keys] * lax.axis_size('ctx')), 'ctx', 0, 0)]
    all_gather x1 -> x0, waiting for transfers between devices: 224 us -> none  [body(): key_piece = lax.all_gather(attn_keys, 'ctx', axis=0, tiled=True)]
    all_gather x1, waiting for transfers between devices: 154 us -> 69.3 us  [body(): value_piece = lax.all_gather(attn_values, 'ctx', axis=0, tiled=True)]
    unnamed x5, local copies, waits for them, and re-layouts: 2.11 us -> 15.6 us
    all_to_all x0 -> x1, starting transfers between devices: none -> 9.35 us  [body(): lax.all_to_all(jnp.stack([attn_keys] * lax.axis_size('ctx')), 'ctx', 0, 0)]
    another operation x0 -> x1, local copies, waits for them, and re-layouts: none -> 6.78 us  [body(): jnp.stack([attn_keys] * lax.axis_size('ctx'))]
  transfers between devices with their start and end apart: 3 -> 3, of which waited for: 3 -> 3; matrix products, arithmetic and copies ran while one was open for 10% -> 13% of each run, Pallas kernels for 0% -> 0%
where the time goes in v2:
time: 598 us; the launch traced here: 597 us
  waiting for transfers between devices  431 us (72%)
  matrix products  73.5 us (12%)
  local copies, waits for them, and re-layouts  43.8 us (7%)
  other arithmetic  25.4 us (4%)
  between operations  13.5 us (2%)
  starting transfers between devices  9.39 us (2%)
    all_to_all x1, waiting for transfers between devices, body(): lax.all_to_all(jnp.stack([attn_keys] * lax.axis_size('ctx')), 'ctx', 0, 0)  309 us
    all_gather x1, waiting for transfers between devices, body(): value_piece = lax.all_gather(attn_values, 'ctx', axis=0, tiled=True)  69.3 us
    reduce_scatter x1, waiting for transfers between devices, body(): lax.psum_scatter(partial_value.astype(jnp.float32).astype(jnp.bfloat16),...  51.9 us
    dot_general x1, matrix products, attend(): jnp.einsum('rhd,phd->hrp', query_set, key_heads, preferred_element_type=j...  31.6 us
    dot_general x1, matrix products, attend(): jnp.einsum('hrp,phd->rhd', weights.astype(jnp.bfloat16), value_heads, pre...  29.6 us
    reduce_sum x1, other arithmetic, attend(): new_sum = jnp.sum(weights, axis=2)  24.2 us
    all_gather x1, local copies, waits for them, and re-layouts, body(): value_piece = lax.all_gather(attn_values, 'ctx', axis=0, tiled=True)  21.4 us
    unnamed x5, local copies, waits for them, and re-layouts  15.6 us
  transfers between devices with their start and end apart: 3, of which 3 were waited for; matrix products, arithmetic and copies ran while one was open for 13% of the time, Pallas kernels for 0%

profile of v2, /device:TPU:1, one launch (start us, length us, event | category | flops | bytes accessed | tf_op | source)
XLA Modules:
  0.0 596.8 jit_solution(12517584107452455145)
XLA Ops:
  6.5 0.0 copy-start
  6.5 0.0 all-gather.2.cloned.1.call-start
  6.5 0.7 all-gather.2.cloned.1.call-update
  7.3 6.8 %stack.2 = bf16[32,256,1024]{2,1,0:T(8,128)(2,1)} broadcast(bf16[256,1024]{1,0:T(8,128)(2,1)} %param.5), dimensions={1,2} | broadcast | bytes 17301504 | tf_op jit(solution)/shard_map/stack | solution.py:51
  14.0 9.3 %all-to-all-start = ((bf16[32,256,1024]{2,1,0:T(8,128)(2,1)}), bf16[32,256,1024]{2,1,0:T(8,128)(2,1)}, u32[]{:S(2)}, u32[]{:S(2)}) async-start(bf16[32,256,1024]{2,1,0:T(8,128)(2,1)} %stack.2), calls=%async_computation | async-start | bytes 33554432 | tf_op jit(solution)/shard_map/all_to_all | solution.py:51
  23.4 0.0 reduce-scatter.2.cloned.1.call-start
  23.5 1.2 broadcast_compare_fusion
  24.7 309.3 %all-to-all-done = bf16[32,256,1024]{2,1,0:T(8,128)(2,1)} async-done(((bf16[32,256,1024]{2,1,0:T(8,128)(2,1)}), bf16[32,256,1024]{2,1,0:T(8,128)(2,1)}, u32[]{:S(2)}, u32[]{:S(2)}) %all-to-all-start) | async-done | bytes 16777248 | tf_op jit(solution)/shard_map/all_to_all | solution.py:51
  334.0 15.6 %copy.11 = bf16[1024,8,8,128]{3,2,1,0:T(8,128)(2,1)} copy(bf16[1024,8,8,128]{3,1,2,0:T(8,128)(2,1)} %bitcast.7) | data formatting | bytes 33554432
  349.7 0.0 copy-done
  349.7 31.6 %fusion = (f32[8,256]{1,0:T(8,128)S(1)}, f32[8,256,8192]{2,1,0:T(8,128)}) fusion(pred[256,8192]{1,0:T(8,128)(4,1)S(1)} %broadcast_compare_fusion, bf16[8192,8,128]{2,1,0:T(8,128)(2,1)} %bitcast.23, bf16[256,1024]{1,0:T(8,128)(2,1)S(1)} %copy-done), kind=kOutput, calls=%fused_computation.2 | convolution fusion | flops 4345296896 | bytes 86515712 | tf_op jit(solution)/shard_map/rhd,phd->hrp/dot_general | solution.py:15
  381.2 24.2 %fusion.1 = f32[8,256]{1,0:T(8,128)S(1)} fusion(f32[8,256,8192]{2,1,0:T(8,128)} %get-tuple-element.6, f32[8,256]{1,0:T(8,128)S(1)} %broadcast_maximum_fusion, pred[256,8192]{1,0:T(8,128)(4,1)S(1)} %broadcast_compare_fusion), kind=kLoop, calls=%fused_computation.3 | loop fusion | flops 83884032 | bytes 69222400 | tf_op jit(solution)/shard_map/reduce_sum | solution.py:21
  405.4 69.3 %all-gather.2.cloned.1.call-done = bf16[8192,1024]{1,0:T(8,128)(2,1)} async-done(((bf16[256,1024]{1,0:T(8,128)(2,1)}), bf16[8192,1024]{1,0:T(8,128)(2,1)}) %all-gather.2.cloned.1.call-update) | async-done | bytes 16777232 | tf_op jit(solution)/shard_map/all_gather | solution.py:53
  474.8 21.4 %copy.9 = bf16[8192,1024]{0,1:T(8,128)(2,1)} copy(bf16[8192,1024]{1,0:T(8,128)(2,1)} %all-gather.2.cloned.1.call-done) | data formatting | bytes 33554432 | tf_op jit(solution)/shard_map/all_gather | solution.py:53
  496.1 0.0 copy-start.1
  496.1 29.6 %divide_convert_fusion = bf16[256,8,128]{0,2,1:T(8,128)(2,1)S(1)} fusion(bf16[8192,8,128]{0,2,1:T(8,128)(2,1)} %bitcast.22, f32[8,256,8192]{2,1,0:T(8,128)} %get-tuple-element.6, f32[8,256]{1,0:T(8,128)S(1)} %broadcast_maximum_fusion, pred[256,8192]{1,0:T(8,128)(4,1)S(1)} %broadcast_compare_fusion, f32[256,8]{0,1:T(8,128)S(1)} %bitcast.25), kind=kOutput, calls=%fused_computation.12 | convolution fusion | flops 4379377664 | bytes 86523904 | tf_op jit(solution)/shard_map/hrp,phd->rhd/dot_general | solution.py:22
  525.8 12.3 %convolution_convert_fusion = bf16[256,8192]{1,0:T(8,128)(2,1)} fusion(bf16[256,1024]{0,1:T(8,128)(2,1)S(1)} %bitcast.24, bf16[1024,8192]{1,0:T(8,128)(2,1)} %param.7), kind=kOutput, calls=%fused_computation.9 | convolution fusion | flops 4297064448 | bytes 21495808 | tf_op jit(solution)/shard_map/dot_general | solution.py:67
  538.0 0.0 reduce-scatter.2.cloned.1.call-update
  538.1 51.9 %reduce-scatter.2.cloned.1.call-done = bf16[256,2048]{1,0:T(8,128)(2,1)} async-done(((bf16[256,8192]{1,0:T(8,128)(2,1)}), bf16[256,2048]{1,0:T(8,128)(2,1)}) %reduce-scatter.2.cloned.1.call-update) | async-done | bytes 1048592 | tf_op jit(solution)/shard_map/reduce_scatter | solution.py:70
  590.0 0.0 copy-done.1
  (4 shorter events, 0.0 us)
Async XLA Ops:
  6.5 343.1 %copy-start = (bf16[256,1024]{1,0:T(8,128)(2,1)S(1)}, bf16[256,1024]{1,0:T(8,128)(2,1)}, u32[]{:S(2)}) copy-start(bf16[256,1024]{1,0:T(8,128)(2,1)} %param.4) | copy-start | bytes 1572868
  6.5 468.2 %all-gather.2.cloned.1.call-start = ((), (), s32[]{:S(2)}) async-start(), calls=%async_computation.2 | async-start | bytes 17301504 | tf_op jit(solution)/shard_map/all_gather | solution.py:53
  14.0 320.0 %all-to-all-start = ((bf16[32,256,1024]{2,1,0:T(8,128)(2,1)}), bf16[32,256,1024]{2,1,0:T(8,128)(2,1)}, u32[]{:S(2)}, u32[]{:S(2)}) async-start(bf16[32,256,1024]{2,1,0:T(8,128)(2,1)} %stack.2), calls=%async_computation | async-start | bytes 33554432 | tf_op jit(solution)/shard_map/all_to_all | solution.py:51
  23.4 566.6 %reduce-scatter.2.cloned.1.call-start = ((), (), s32[]{:S(2)}) async-start(), calls=%async_computation.3 | async-start | bytes 5242880 | tf_op jit(solution)/shard_map/reduce_scatter | solution.py:70
  496.1 93.8 %copy-start.1 = (bf16[256,1024]{1,0:T(8,128)(2,1)S(1)}, bf16[256,1024]{1,0:T(8,128)(2,1)}, u32[]{:S(2)}) copy-start(bf16[256,1024]{1,0:T(8,128)(2,1)} %param.4) | copy-start | bytes 1572868
Sparse Core Ops, SparseCore 0:
  9.0 465.7 all-gather.1
  538.2 51.7 reduce-scatter.1
